TPU v7x, 32 devices: a whole 2x2x4 slice. The times are simulated.
32 devices in a mesh: head: 2 (over x), seq: 16 (over z, y, core).
Axes of the slice: x: 2, y: 2, z: 4, core: 2. Of those that a mesh axis runs over, the one named last changes fastest.
Arguments:
- queries: bfloat16 [2, 1024, 4096], P(None, 'seq', 'head'), may hold values from -256 to 256
- keys: bfloat16 [2, 1024, 4096], P(None, 'seq', 'head'), may hold values from -256 to 256
- values: bfloat16 [2, 1024, 4096], P(None, 'seq', 'head'), may hold values from -6 to 6
- token_rates: float32 [1, 16, 1024], P(None, 'head', 'seq'), may hold values from 0.1 to 1
- step_size: float32 [16], P('head'), may hold values from 0.3 to 1
- w_gate: bfloat16 [16, 256, 512], P('head', 'seq'), may hold values from -0.375 to 0.375
- w_up: bfloat16 [16, 256, 512], P('head', 'seq'), may hold values from -0.375 to 0.375
- w_down: bfloat16 [16, 512, 256], P('head', 'seq'), may hold values from -0.25 to 0.25
- norm_gain: float32 [4096], replicated, may hold values from 0.5 to 1.5
Outputs:
- mixed: bfloat16 [2, 1024, 4096], P(None, ('seq', 'head'))
All inputs are finite; a program needn't handle non-finite values.
Results may differ from a plain program's by a relative error of at most 0.0095.
Values may be sent and summed in bfloat16 or wider, within the bound.
A program may use at most 128 MiB of HBM per device.

v0:
```python
import math

import jax
import jax.numpy as jnp
from jax import lax
from jax.sharding import PartitionSpec as P

DH = 256
DF = 512
WIN = 512
NS_STEPS = 5


def spread(block, axis, holder):
    block = jnp.where(lax.axis_index(axis) == holder, block, jnp.zeros_like(block))
    return lax.psum(block, axis)


def shifted(array, axis, by):
    count = lax.axis_size(axis)
    return lax.ppermute(array, axis, [(i, (i + by) % count) for i in range(count)])


def rms_norm(values_in):
    wide = values_in.astype(jnp.float32)
    mean_square = jnp.mean(wide * wide, axis=-1, keepdims=True)
    return (wide * lax.rsqrt(mean_square + 1e-06)).astype(jnp.bfloat16)


def newton(grad_in):
    norm_value = jnp.sqrt(jnp.sum(grad_in * grad_in))
    iterate = grad_in / (norm_value + 1e-07)
    for _ in range(NS_STEPS):
        gram = jnp.dot(
            iterate, iterate.T, precision=lax.Precision.HIGHEST, preferred_element_type=jnp.float32
        )
        poly = -4.775 * gram + 2.0315 * jnp.dot(
            gram, gram, precision=lax.Precision.HIGHEST, preferred_element_type=jnp.float32
        )
        iterate = 3.4445 * iterate + jnp.dot(
            poly, iterate, precision=lax.Precision.HIGHEST, preferred_element_type=jnp.float32
        )
    return iterate


def orthogonalize(summed, seq_count, seq_index):
    problems = summed.shape[0]
    stride = 1
    per_device = -(-problems // seq_count)
    owned = []
    for slot_index in range(per_device):
        problem = jnp.clip(seq_index // stride + slot_index * seq_count, 0, problems - 1)
        owned.append(newton(lax.dynamic_index_in_dim(summed, problem, 0, keepdims=False)))
    results = []
    for problem_index in range(problems):
        results.append(
            spread(
                owned[problem_index // seq_count].astype(jnp.bfloat16),
                "seq",
                problem_index % seq_count * stride,
            ).astype(jnp.float32)
        )
    return jnp.stack(results)


def body(queries, keys, values, token_rates, step_size, w_gate, w_up, w_down, norm_gain):
    blocks_here, tok_rows, width_here = queries.shape
    head_count = width_here // DH
    seq_count = lax.axis_size("seq")
    seq_index = lax.axis_index("seq")
    gate_fast, up_fast, down_fast = (
        lax.all_gather(w_gate, "seq", axis=1, tiled=True),
        lax.all_gather(w_up, "seq", axis=1, tiled=True),
        lax.all_gather(w_down, "seq", axis=1, tiled=True),
    )
    reach_count = -(-WIN // tok_rows)
    earlier_blocks = []
    passed = (keys, values)
    for distance in range(1, reach_count + 1):
        arrived = shifted((passed[0], passed[1]), "seq", 1)
        passed = arrived
        settled = []
        for part_arr in arrived:
            before = jnp.concatenate([jnp.zeros_like(part_arr[:1]), part_arr[:-1]], 0)
            settled.append(jnp.where(seq_index >= distance, part_arr, before))
        earlier_blocks.insert(0, settled)
    context_keys = jnp.concatenate([pair_item[0] for pair_item in earlier_blocks] + [keys], 1)
    context_values = jnp.concatenate([pair_item[1] for pair_item in earlier_blocks] + [values], 1)
    context_len = context_keys.shape[1]
    context_keys = context_keys.reshape(blocks_here, context_len, head_count, DH)
    context_values = context_values.reshape(blocks_here, context_len, head_count, DH)
    query_heads = queries.reshape(blocks_here, tok_rows, head_count, DH)
    key_heads = keys.reshape(blocks_here, tok_rows, head_count, DH)
    value_heads = values.reshape(blocks_here, tok_rows, head_count, DH)
    scores = jnp.einsum(
        "bihd,bjhd->bhij", query_heads, context_keys, preferred_element_type=jnp.float32
    ) * (1.0 / math.sqrt(DH))
    query_rows = jnp.arange(tok_rows, dtype=jnp.int32)
    key_rows = jnp.arange(context_len, dtype=jnp.int32)
    row_gap = reach_count * tok_rows + query_rows[:, None] - key_rows[None, :]
    block_ids = jnp.arange(blocks_here, dtype=jnp.int32)
    key_pos = (
        block_ids[:, None] * (tok_rows * seq_count)
        + seq_index * tok_rows
        - reach_count * tok_rows
        + key_rows[None, :]
    )
    allowed = ((row_gap >= 0) & (row_gap < WIN))[None, :, :] & (key_pos >= 0)[:, None, :]
    scores = jnp.where(allowed[:, None, :, :], scores, -1e30)
    row_top = jnp.max(scores, axis=-1, keepdims=True)
    exp_scores = jnp.exp(scores - row_top)
    attn_weights = (exp_scores / jnp.sum(exp_scores, axis=-1, keepdims=True)).astype(jnp.bfloat16)
    attention = jnp.einsum(
        "bhij,bjhd->bihd", attn_weights, context_values, preferred_element_type=jnp.float32
    )
    query_norm = rms_norm(query_heads)
    key_norm = rms_norm(key_heads[: blocks_here - 1])
    fast_parts = []
    for block_index in range(blocks_here):
        gate_query = jnp.einsum(
            "thd,hdf->htf", query_norm[block_index], gate_fast, preferred_element_type=jnp.float32
        )
        up_query = jnp.einsum(
            "thd,hdf->htf", query_norm[block_index], up_fast, preferred_element_type=jnp.float32
        )
        hidden = (jax.nn.silu(gate_query) * up_query).astype(jnp.bfloat16)
        fast_parts.append(
            jnp.einsum("htf,hfd->thd", hidden, down_fast, preferred_element_type=jnp.float32)
        )
        if block_index < blocks_here - 1:
            keys_now = key_norm[block_index]
            vals_now = value_heads[block_index]
            gate_pre = jnp.einsum(
                "thd,hdf->htf", keys_now, gate_fast, preferred_element_type=jnp.float32
            )
            up_pre = jnp.einsum(
                "thd,hdf->htf", keys_now, up_fast, preferred_element_type=jnp.float32
            )
            back = jnp.einsum(
                "thd,hfd->htf", vals_now, down_fast, preferred_element_type=jnp.float32
            )
            rate_col = token_rates[block_index][:, :, None]
            sigmoid_val = jax.nn.sigmoid(gate_pre)
            act_val = gate_pre * sigmoid_val
            d_gate = (
                rate_col * back * up_pre * sigmoid_val * (1.0 + gate_pre * (1.0 - sigmoid_val))
            ).astype(jnp.bfloat16)
            d_up = (rate_col * back * act_val).astype(jnp.bfloat16)
            h_rate = (rate_col * act_val * up_pre).astype(jnp.bfloat16)
            grad_gate = jnp.einsum(
                "thd,htf->hdf", keys_now, d_gate, preferred_element_type=jnp.float32
            )
            grad_up = jnp.einsum("thd,htf->hdf", keys_now, d_up, preferred_element_type=jnp.float32)
            grad_down_t = jnp.einsum(
                "thd,htf->hdf", vals_now, h_rate, preferred_element_type=jnp.float32
            )
            stacked = jnp.stack([grad_gate, grad_up, grad_down_t], 1).reshape(
                head_count * 3, DH, DF
            )
            summed = lax.psum(stacked, "seq")
            orthogonal = orthogonalize(summed, seq_count, seq_index).reshape(head_count, 3, DH, DF)
            step_col = step_size[:, None, None]
            gate_fast = (gate_fast.astype(jnp.float32) + step_col * orthogonal[:, 0]).astype(
                jnp.bfloat16
            )
            up_fast = (up_fast.astype(jnp.float32) + step_col * orthogonal[:, 1]).astype(
                jnp.bfloat16
            )
            down_fast = (
                down_fast.astype(jnp.float32) + step_col * jnp.swapaxes(orthogonal[:, 2], 1, 2)
            ).astype(jnp.bfloat16)
    fast_out = jnp.stack(fast_parts)
    combined = (
        (fast_out + attention).astype(jnp.bfloat16).reshape(blocks_here, tok_rows, width_here)
    )
    wide = lax.all_to_all(combined, "head", split_axis=1, concat_axis=2, tiled=True).astype(
        jnp.float32
    )
    mean_square = jnp.mean(wide * wide, axis=-1, keepdims=True)
    return (wide * lax.rsqrt(mean_square + 1e-06) * norm_gain).astype(jnp.bfloat16)


def solution(mesh):
    placed = (
        P(None, "seq", "head"),
        P(None, "seq", "head"),
        P(None, "seq", "head"),
        P(None, "head", "seq"),
        P("head"),
        P("head", "seq", None),
        P("head", "seq", None),
        P("head", "seq", None),
        P(),
    )
    return jax.shard_map(
        body, mesh=mesh, in_specs=placed, out_specs=P(None, ("seq", "head"), None), check_vma=False
    )
```

profile of v0, /device:TPU:25, one launch (start us, length us, event | category | flops | bytes accessed | tf_op | source)
XLA Modules:
  0.0 677.8 jit_solution(11501068691853412412)
XLA Ops:
  11.0 6.3 collective-permute-done.8
  19.7 4.6 collective-permute-done
  26.7 3.1 collective-permute-done.9
  32.3 3.1 collective-permute-done.1
  35.4 2.5 collective-permute-start.2
  43.5 3.1 collective-permute-done.2
  52.3 2.6 collective-permute-start.12
  54.9 6.4 collective-permute-done.3
  65.3 4.0 collective-permute-done.12
  71.7 3.0 collective-permute-done.4
  74.8 2.6 collective-permute-start.5
  77.3 4.3 copy.76
  81.7 38.0 %all-gather.4.cloned.1.call-done = bf16[8,256,512]{2,1,0:T(8,128)(2,1)} async-done(((bf16[8,16,512]{2,1,0:T(8,128)(2,1)}), bf16[8,256,512]{2,1,0:T(8,128)(2,1)}) %all-gather.4.cloned.1.call-update) | async-done | bytes 2097168 | tf_op jit(solution)/shard_map/all_gather | solution.py:72
  123.8 2.7 convolution_bitcast_fusion.1
  126.5 35.6 %all-gather.6.cloned.1.call-done = bf16[8,256,512]{2,1,0:T(8,128)(2,1)} async-done(((bf16[8,16,512]{2,1,0:T(8,128)(2,1)}), bf16[8,256,512]{2,1,0:T(8,128)(2,1)}) %all-gather.6.cloned.1.call-update) | async-done | bytes 2097168 | tf_op jit(solution)/shard_map/all_gather | solution.py:73
  164.2 2.8 convolution_bitcast_fusion.2
  166.9 2.8 convolution_bitcast_fusion
  170.1 10.1 %pad_maximum_fusion = f32[8,3,256,512]{3,2,0,1:T(8,128)} fusion(f32[8,1,256,512]{3,2,0,1:T(8,128)} %convolution_bitcast_fusion, f32[8,1,256,512]{3,2,0,1:T(8,128)S(1)} %copy-done.2, f32[8,1,256,512]{3,2,0,1:T(8,128)} %convolution_bitcast_fusion.2), kind=kLoop, calls=%fused_computation.1 | loop fusion | flops 6291456 | bytes 25165824 | tf_op jit(solution)/shard_map/stack | solution.py:157
  180.2 11.4 %copy.83 = f32[8,3,256,512]{3,2,1,0:T(8,128)} copy(f32[8,3,256,512]{3,2,0,1:T(8,128)} %pad_maximum_fusion) | data formatting | bytes 25165824 | tf_op jit(solution)/shard_map/stack | solution.py:157
  217.8 2.6 collective-permute-start.7
  223.6 4.6 fusion.48
  229.2 3.1 collective-permute-done.7
  249.8 192.0 %all-reduce.20.cloned.1.call-done = f32[24,256,512]{2,1,0:T(8,128)} async-done(((f32[24,256,512]{2,1,0:T(8,128)}), f32[24,256,512]{2,1,0:T(8,128)}) %all-reduce.20.cloned.1.call-update) | async-done | bytes 12582928 | tf_op jit(solution)/shard_map/psum | solution.py:160
  466.4 3.4 select_bitcast_fusion
  479.7 3.8 fusion.4
  485.9 137.6 %all-reduce.22.cloned.1.call-done = (bf16[1,256,512]{2,1,0:T(8,128)(2,1)}, bf16[1,256,512]{2,1,0:T(8,128)(2,1)}, bf16[1,256,512]{2,1,0:T(8,128)(2,1)}, bf16[1,25...) async-done(((bf16[1,256,512]{2,1,0:T(8,128)(2,1)}, ...) | async-done | bytes 6291472 | tf_op jit(solution)/shard_map/psum | solution.py:16
  633.4 2.7 copy-done.3
  636.1 4.6 convert.30
  640.6 4.6 copy-done
  647.1 6.8 fusion.49
  653.8 5.1 fusion.40
  659.4 9.8 %all_to_all.4 = bf16[2,64,2048]{2,0,1:T(2,128)(2,1)S(1)} all-to-all(bf16[2,64,2048]{2,0,1:T(2,128)(2,1)S(1)} %reshape.169), channel_id=1, replica_groups=mesh['head'=2,'seq'=16] {'head'}, dimensions={1} | all-to-all | bytes 1048576 | tf_op jit(solution)/shard_map/all_to_all | solution.py:176
  (249 shorter events, 132.1 us)
Async XLA Ops:
  6.5 70.8 %all-gather.8.cloned.1.call-start = ((), (), s32[]{:S(2)}) async-start(), calls=%async_computation.3 | async-start | bytes 2228224 | tf_op jit(solution)/shard_map/all_gather | solution.py:74
  8.2 111.5 %all-gather.4.cloned.1.call-start = ((), (), s32[]{:S(2)}) async-start(), calls=%async_computation.1 | async-start | bytes 2228224 | tf_op jit(solution)/shard_map/all_gather | solution.py:72
  8.9 153.1 %all-gather.6.cloned.1.call-start = ((), (), s32[]{:S(2)}) async-start(), calls=%async_computation.2 | async-start | bytes 2228224 | tf_op jit(solution)/shard_map/all_gather | solution.py:73
  9.0 8.3 %collective-permute-start.8 = (bf16[2,64,2048]{2,1,0:T(8,128)(2,1)}, bf16[2,64,2048]{2,1,0:T(8,128)(2,1)S(1)}, u32[]{:S(2)}, u32[]{:S(2)}) collective-permute-start(bf16[2,64,2048]{2,1,0:T(8,128)(2,1)} %param.10), channel_id=1, source_target_pairs={{0,1},{1,2},{2,3},{3,4},{4,5},{5,6},{6,7},{7,8},{8,9},{9,10},{10,1... | collective-permute-start | bytes 1572872 | tf_op jit(solution)/shard_map/ppermute | solution.py:21
  10.8 13.5 %collective-permute-start = (bf16[2,64,2048]{2,1,0:T(8,128)(2,1)}, bf16[2,64,2048]{2,1,0:T(8,128)(2,1)S(1)}, u32[]{:S(2)}, u32[]{:S(2)}) collective-permute-start(bf16[2,64,2048]{2,1,0:T(8,128)(2,1)} %param.11), channel_id=1, source_target_pairs={{0,1},{1,2},{2,3},{3,4},{4,5},{5,6},{6,7},{7,8},{8,9},{9,10},{10,1... | collective-permute-start | bytes 1572872 | tf_op jit(solution)/shard_map/ppermute | solution.py:21
  10.9 430.9 %all-reduce.20.cloned.1.call-start = ((), (), s32[]{:S(2)}) async-start(), calls=%async_computation.4 | async-start | bytes 25165824 | tf_op jit(solution)/shard_map/psum | solution.py:160
  17.3 18.2 %copy-start.11 = (bf16[2,64,2048]{2,1,0:T(8,128)(2,1)}, bf16[2,64,2048]{2,1,0:T(8,128)(2,1)S(1)}, u32[]{:S(2)}) copy-start(bf16[2,64,2048]{2,1,0:T(8,128)(2,1)S(1)} %collective-permute-done.8) | copy-start | bytes 1572868
  17.3 12.5 %collective-permute-start.9 = (bf16[2,64,2048]{2,1,0:T(8,128)(2,1)S(1)}, bf16[2,64,2048]{2,1,0:T(8,128)(2,1)S(1)}, u32[]{:S(2)}, u32[]{:S(2)}) collective-permute-start(bf16[2,64,2048]{2,1,0:T(8,128)(2,1)S(1)} %collective-permute-done.8), channel_id=1, source_target_pairs={{0,1},{1,2},{2,3},{3,4},{4,5},{5,6},{6,7},{7,8},{8,9},{9,10},{10,1... | collective-permute-start | bytes 1572872 | tf_op jit(solution)/shard_map/ppermute | solution.py:21
  24.3 14.6 %copy-start.9 = (bf16[2,64,2048]{2,1,0:T(8,128)(2,1)}, bf16[2,64,2048]{2,1,0:T(8,128)(2,1)S(1)}, u32[]{:S(2)}) copy-start(bf16[2,64,2048]{2,1,0:T(8,128)(2,1)S(1)} %collective-permute-done) | copy-start | bytes 1572868
  24.3 11.1 %collective-permute-start.1 = (bf16[2,64,2048]{2,1,0:T(8,128)(2,1)S(1)}, bf16[2,64,2048]{2,1,0:T(8,128)(2,1)S(1)}, u32[]{:S(2)}, u32[]{:S(2)}) collective-permute-start(bf16[2,64,2048]{2,1,0:T(8,128)(2,1)S(1)} %collective-permute-done), channel_id=1, source_target_pairs={{0,1},{1,2},{2,3},{3,4},{4,5},{5,6},{6,7},{7,8},{8,9},{9,10},{10,1... | collective-permute-start | bytes 1572872 | tf_op jit(solution)/shard_map/ppermute | solution.py:21
  29.8 34.9 %copy-start.16 = (bf16[2,64,2048]{2,1,0:T(8,128)(2,1)}, bf16[2,64,2048]{2,1,0:T(8,128)(2,1)S(1)}, u32[]{:S(2)}) copy-start(bf16[2,64,2048]{2,1,0:T(8,128)(2,1)S(1)} %collective-permute-done.9) | copy-start | bytes 1572868
  29.8 11.2 %collective-permute-start.10 = (bf16[2,64,2048]{2,1,0:T(8,128)(2,1)S(1)}, bf16[2,64,2048]{2,1,0:T(8,128)(2,1)S(1)}, u32[]{:S(2)}, u32[]{:S(2)}) collective-permute-start(bf16[2,64,2048]{2,1,0:T(8,128)(2,1)S(1)} %collective-permute-done.9), channel_id=1, source_target_pairs={{0,1},{1,2},{2,3},{3,4},{4,5},{5,6},{6,7},{7,8},{8,9},{9,10},{10,1... | collective-permute-start | bytes 1572872 | tf_op jit(solution)/shard_map/ppermute | solution.py:21
  35.4 46.2 %copy-start.12 = (bf16[2,64,2048]{2,1,0:T(8,128)(2,1)}, bf16[2,64,2048]{2,1,0:T(8,128)(2,1)S(1)}, u32[]{:S(2)}) copy-start(bf16[2,64,2048]{2,1,0:T(8,128)(2,1)S(1)} %collective-permute-done.1) | copy-start | bytes 1572868
  35.4 11.2 %collective-permute-start.2 = (bf16[2,64,2048]{2,1,0:T(8,128)(2,1)S(1)}, bf16[2,64,2048]{2,1,0:T(8,128)(2,1)S(1)}, u32[]{:S(2)}, u32[]{:S(2)}) collective-permute-start(bf16[2,64,2048]{2,1,0:T(8,128)(2,1)S(1)} %collective-permute-done.1), channel_id=1, source_target_pairs={{0,1},{1,2},{2,3},{3,4},{4,5},{5,6},{6,7},{7,8},{8,9},{9,10},{10,1... | collective-permute-start | bytes 1572872 | tf_op jit(solution)/shard_map/ppermute | solution.py:21
  41.1 23.7 %copy-start.18 = (bf16[2,64,2048]{2,1,0:T(8,128)(2,1)}, bf16[2,64,2048]{2,1,0:T(8,128)(2,1)S(1)}, u32[]{:S(2)}) copy-start(bf16[2,64,2048]{2,1,0:T(8,128)(2,1)S(1)} %collective-permute-done.10) | copy-start | bytes 1572868
  41.1 11.2 %collective-permute-start.11 = (bf16[2,64,2048]{2,1,0:T(8,128)(2,1)S(1)}, bf16[2,64,2048]{2,1,0:T(8,128)(2,1)}, u32[]{:S(2)}, u32[]{:S(2)}) collective-permute-start(bf16[2,64,2048]{2,1,0:T(8,128)(2,1)S(1)} %collective-permute-done.10), channel_id=1, source_target_pairs={{0,1},{1,2},{2,3},{3,4},{4,5},{5,6},{6,7},{7,8},{8,9},{9,10},{10,1... | collective-permute-start | bytes 1572872 | tf_op jit(solution)/shard_map/ppermute | solution.py:21
  46.7 75.0 %copy-start.14 = (bf16[2,64,2048]{2,1,0:T(8,128)(2,1)}, bf16[2,64,2048]{2,1,0:T(8,128)(2,1)S(1)}, u32[]{:S(2)}) copy-start(bf16[2,64,2048]{2,1,0:T(8,128)(2,1)S(1)} %collective-permute-done.2) | copy-start | bytes 1572868
  46.7 14.6 %collective-permute-start.3 = (bf16[2,64,2048]{2,1,0:T(8,128)(2,1)S(1)}, bf16[2,64,2048]{2,1,0:T(8,128)(2,1)S(1)}, u32[]{:S(2)}, u32[]{:S(2)}) collective-permute-start(bf16[2,64,2048]{2,1,0:T(8,128)(2,1)S(1)} %collective-permute-done.2), channel_id=1, source_target_pairs={{0,1},{1,2},{2,3},{3,4},{4,5},{5,6},{6,7},{7,8},{8,9},{9,10},{10,1... | collective-permute-start | bytes 1572872 | tf_op jit(solution)/shard_map/ppermute | solution.py:21
  52.3 17.0 %collective-permute-start.12 = (bf16[2,64,2048]{2,1,0:T(8,128)(2,1)}, bf16[2,64,2048]{2,1,0:T(8,128)(2,1)}, u32[]{:S(2)}, u32[]{:S(2)}) collective-permute-start(bf16[2,64,2048]{2,1,0:T(8,128)(2,1)} %collective-permute-done.11), channel_id=1, source_target_pairs={{0,1},{1,2},{2,3},{3,4},{4,5},{5,6},{6,7},{7,8},{8,9},{9,10},{10,1... | collective-permute-start | bytes 1572872 | tf_op jit(solution)/shard_map/ppermute | solution.py:21
  61.3 20.4 %copy-start.15 = (bf16[2,64,2048]{2,1,0:T(8,128)(2,1)}, bf16[2,64,2048]{2,1,0:T(8,128)(2,1)S(1)}, u32[]{:S(2)}) copy-start(bf16[2,64,2048]{2,1,0:T(8,128)(2,1)S(1)} %collective-permute-done.3) | copy-start | bytes 1572868
  61.3 13.5 %collective-permute-start.4 = (bf16[2,64,2048]{2,1,0:T(8,128)(2,1)S(1)}, bf16[2,64,2048]{2,1,0:T(8,128)(2,1)}, u32[]{:S(2)}, u32[]{:S(2)}) collective-permute-start(bf16[2,64,2048]{2,1,0:T(8,128)(2,1)S(1)} %collective-permute-done.3), channel_id=1, source_target_pairs={{0,1},{1,2},{2,3},{3,4},{4,5},{5,6},{6,7},{7,8},{8,9},{9,10},{10,1... | collective-permute-start | bytes 1572872 | tf_op jit(solution)/shard_map/ppermute | solution.py:21
  64.9 56.8 %copy-start.47 = (f32[1,8,64]{2,1,0:T(8,128)S(1)}, f32[1,8,64]{2,1,0:T(8,128)}, u32[]{:S(2)}) copy-start(f32[1,8,64]{2,1,0:T(8,128)} %param.12) | copy-start | bytes 6148
  69.2 122.5 %collective-permute-start.13 = (bf16[2,64,2048]{2,1,0:T(8,128)(2,1)}, bf16[2,64,2048]{2,1,0:T(8,128)(2,1)}, u32[]{:S(2)}, u32[]{:S(2)}) collective-permute-start(bf16[2,64,2048]{2,1,0:T(8,128)(2,1)} %collective-permute-done.12), channel_id=1, source_target_pairs={{0,1},{1,2},{2,3},{3,4},{4,5},{5,6},{6,7},{7,8},{8,9},{9,10},{10,1... | collective-permute-start | bytes 1572872 | tf_op jit(solution)/shard_map/ppermute | solution.py:21
  74.8 117.4 %collective-permute-start.5 = (bf16[2,64,2048]{2,1,0:T(8,128)(2,1)}, bf16[2,64,2048]{2,1,0:T(8,128)(2,1)}, u32[]{:S(2)}, u32[]{:S(2)}) collective-permute-start(bf16[2,64,2048]{2,1,0:T(8,128)(2,1)} %collective-permute-done.4), channel_id=1, source_target_pairs={{0,1},{1,2},{2,3},{3,4},{4,5},{5,6},{6,7},{7,8},{8,9},{9,10},{10,1... | collective-permute-start | bytes 1572872 | tf_op jit(solution)/shard_map/ppermute | solution.py:21
  191.6 30.5 %copy-start.1 = (bf16[8,256,512]{2,1,0:T(8,128)(2,1)S(1)}, bf16[8,256,512]{2,1,0:T(8,128)(2,1)}, u32[]{:S(2)}) copy-start(bf16[8,256,512]{2,1,0:T(8,128)(2,1)} %all-gather.4.cloned.1.call-done) | copy-start | bytes 6291460
  191.6 431.9 %all-reduce.22.cloned.1.call-start = ((), (), s32[]{:S(2)}) async-start(), calls=%async_computation.5 | async-start | bytes 12582912 | tf_op jit(solution)/shard_map/psum | solution.py:16
  191.7 20.7 %collective-permute-start.14 = (bf16[2,64,2048]{2,1,0:T(8,128)(2,1)}, bf16[2,64,2048]{2,1,0:T(8,128)(2,1)}, u32[]{:S(2)}, u32[]{:S(2)}) collective-permute-start(bf16[2,64,2048]{2,1,0:T(8,128)(2,1)} %collective-permute-done.13), channel_id=1, source_target_pairs={{0,1},{1,2},{2,3},{3,4},{4,5},{5,6},{6,7},{7,8},{8,9},{9,10},{10,1... | collective-permute-start | bytes 1572872 | tf_op jit(solution)/shard_map/ppermute | solution.py:21
  192.2 25.6 %collective-permute-start.6 = (bf16[2,64,2048]{2,1,0:T(8,128)(2,1)}, bf16[2,64,2048]{2,1,0:T(8,128)(2,1)}, u32[]{:S(2)}, u32[]{:S(2)}) collective-permute-start(bf16[2,64,2048]{2,1,0:T(8,128)(2,1)} %collective-permute-done.5), channel_id=1, source_target_pairs={{0,1},{1,2},{2,3},{3,4},{4,5},{5,6},{6,7},{7,8},{8,9},{9,10},{10,1... | collective-permute-start | bytes 1572872 | tf_op jit(solution)/shard_map/ppermute | solution.py:21
  192.9 30.7 %copy-start.7 = (bf16[2,64,8,256]{3,1,2,0:T(8,128)(2,1)}, bf16[2,64,8,256]{3,1,2,0:T(8,128)(2,1)S(1)}, u32[]{:S(2)}) copy-start(bf16[2,64,8,256]{3,1,2,0:T(8,128)(2,1)S(1)} %fusion.67) | copy-start | bytes 1572868
  212.5 15.7 %collective-permute-start.15 = (bf16[2,64,2048]{2,1,0:T(8,128)(2,1)}, bf16[2,64,2048]{2,1,0:T(8,128)(2,1)}, u32[]{:S(2)}, u32[]{:S(2)}) collective-permute-start(bf16[2,64,2048]{2,1,0:T(8,128)(2,1)} %collective-permute-done.14), channel_id=1, source_target_pairs={{0,1},{1,2},{2,3},{3,4},{4,5},{5,6},{6,7},{7,8},{8,9},{9,10},{10,1... | collective-permute-start | bytes 1572872 | tf_op jit(solution)/shard_map/ppermute | solution.py:21
  217.8 14.5 %collective-permute-start.7 = (bf16[2,64,2048]{2,1,0:T(8,128)(2,1)}, bf16[2,64,2048]{2,1,0:T(8,128)(2,1)}, u32[]{:S(2)}, u32[]{:S(2)}) collective-permute-start(bf16[2,64,2048]{2,1,0:T(8,128)(2,1)} %collective-permute-done.6), channel_id=1, source_target_pairs={{0,1},{1,2},{2,3},{3,4},{4,5},{5,6},{6,7},{7,8},{8,9},{9,10},{10,1... | collective-permute-start | bytes 1572872 | tf_op jit(solution)/shard_map/ppermute | solution.py:21
  228.2 14.1 %copy-start.26 = (bf16[1,64,2048]{2,1,0:T(8,128)(2,1)S(1)}, bf16[1,64,2048]{2,1,0:T(8,128)(2,1)}, u32[]{:S(2)}) copy-start(bf16[1,64,2048]{2,1,0:T(8,128)(2,1)} %slice.104) | copy-start | bytes 786436
  (39 other events, 312.1 us)
Sparse Core Ops, SparseCore 0:
  9.5 64.7 all-gather.7
  76.5 43.0 all-gather.3
  121.8 40.1 all-gather.5
  191.7 250.0 all-reduce.19
  470.0 153.5 all-reduce.21
where the time goes:
time: 690 us; the launch traced here: 678 us
  waiting for transfers between devices  445 us (64%)
  local copies, waits for them, and re-layouts  64.8 us (9%)
  matrix products  62.4 us (9%)
  other arithmetic  47.5 us (7%)
  starting transfers between devices  32.6 us (5%)
  between operations  15.9 us (2%)
  blocking collectives  9.84 us (1%)
    psum x1, waiting for transfers between devices, body(): summed = lax.psum(stacked, 'seq')  192 us
    psum x1, waiting for transfers between devices, spread(): return lax.psum(block, axis)  138 us
    ppermute x16, waiting for transfers between devices, shifted(): lax.ppermute(array, axis, [(i, (i + by) % count) for i in range(count)])  40.6 us
    all_gather x1, waiting for transfers between devices, body(): lax.all_gather(w_gate, 'seq', axis=1, tiled=True)  38 us
    all_gather x1, waiting for transfers between devices, body(): lax.all_gather(w_up, 'seq', axis=1, tiled=True)  35.6 us
    ppermute x16, starting transfers between devices, shifted(): lax.ppermute(array, axis, [(i, (i + by) % count) for i in range(count)])  32.5 us
    slice x16, local copies, waits for them, and re-layouts, body(): before = jnp.concatenate([jnp.zeros_like(part_arr[:1]), part_arr[:-1]], 0)  25 us
    unnamed x15, other arithmetic  24.5 us
  transfers between devices with their start and end apart: 21, of which 16 were waited for; matrix products, arithmetic and copies ran while one was open for 16% of the time, Pallas kernels for 0%

commit v1 on v0

v1 whole, which is shorter than its diff:
```python
import functools
import math

import jax
import jax.numpy as jnp
from jax import lax
from jax.experimental import pallas as pl
from jax.experimental.pallas import tpu as pltpu
from jax.sharding import PartitionSpec as P

DH = 256
DF = 512
WIN = 512
NS_STEPS = 5
TILE = 256
F32 = jnp.float32
BF16 = jnp.bfloat16
NN = (((1,), (0,)), ((), ()))
NT = (((1,), (1,)), ((), ()))
TN = (((0,), (0,)), ((), ()))

K0, V0, WG, WU, WD, RATE, QQ0, QQ1, K1, V1 = range(10)
FIRST = (K0, V0, WG, WU, WD, RATE)
FIN = 10


def dot(a, b, dims=NN):
    return lax.dot_general(a, b, dims, preferred_element_type=F32)


def split(a):
    high = a.astype(BF16)
    return high, (a - high.astype(F32)).astype(BF16)


def dot3(a, b, dims=NN):
    return dot(a[0], b[0], dims) + (dot(a[0], b[1], dims) + dot(a[1], b[0], dims))


def rms(tile):
    wide = tile.astype(F32)
    mean_square = jnp.mean(wide * wide, axis=-1, keepdims=True)
    return (wide * lax.rsqrt(mean_square + 1e-06)).astype(BF16)


def kernel(cfg, *refs):
    heads_here, seq_count, head_devices, tok, length, gathered, out_type = cfg
    (q_in, k_in, v_in, rate_in, step_in, wg_in, wu_in, wd_in, gain_in, out_ref) = refs[:10]
    (kbuf, vbuf, qbuf, wg, wu, wd, rates, rate_col, grads, obuf, fin) = refs[10:21]
    send, recv, fwd_send, out_send = refs[21:]
    per_head = seq_count // heads_here
    x = lax.axis_index("head")
    s = lax.axis_index("seq")
    my_head = s // per_head
    member = s % per_head
    rows = tok // head_devices
    g_rows = DH // seq_count
    d_rows = DF // seq_count

    def at_rows(ref, start, size, step):
        return ref.at[pl.ds(pl.multiple_of(start, step), size)]

    def column(ref, block, h):
        return ref.at[block, :, pl.ds(pl.multiple_of(h * DH, DH), DH)]

    def routes(h, which):
        start = s * tok
        if which == K0:
            return column(k_in, 0, h), at_rows(kbuf, WIN + start, tok, tok), 1
        if which == V0:
            return column(v_in, 0, h), at_rows(vbuf, WIN + start, tok, tok), 1
        if which == WG:
            return wg_in.at[h], at_rows(wg, s * g_rows, g_rows, g_rows), 1
        if which == WU:
            return wu_in.at[h], at_rows(wu, s * g_rows, g_rows, g_rows), 1
        if which == WD:
            return wd_in.at[h], at_rows(wd, s * d_rows, d_rows, d_rows), 1
        if which == RATE:
            return rate_in.at[h], rates.at[s], 1
        if which == QQ0:
            return column(q_in, 0, h), at_rows(qbuf, start, tok, tok), 0
        if which == QQ1:
            return column(q_in, 1, h), at_rows(qbuf, start, tok, tok), 1
        if which == K1:
            return column(k_in, 1, h), at_rows(kbuf, WIN + length + start, tok, tok), 1
        return column(v_in, 1, h), at_rows(vbuf, WIN + length + start, tok, tok), 1

    def recv_of(which):
        return recv.at[QQ0 if which == QQ1 else which]

    def each(which_list, action):
        def one(j, carry):
            h = (my_head + j) % heads_here
            for which in which_list:
                if gathered and which in (WG, WU, WD):
                    continue
                src, dst, role = routes(h, which)
                dest = h * per_head + role
                remote = pltpu.make_async_remote_copy(
                    src, dst, send.at[which, h], recv_of(which),
                    device_id=(x, dest), device_id_type=pl.DeviceIdType.MESH,
                )
                if action == "start":

                    @pl.when(dest == s)
                    def _():
                        pltpu.make_async_copy(src, dst, recv_of(which)).start()

                    @pl.when(dest != s)
                    def _():
                        remote.start()
                else:

                    @pl.when(dest != s)
                    def _():
                        remote.wait_send()
            return carry

        lax.fori_loop(0, heads_here, one, 0)

    def arrived(ref, sem):
        pltpu.make_async_copy(ref, ref, sem).wait()

    first_block = pl.ds(WIN, length)
    second_block = pl.ds(WIN + length, length)
    owner = member < 2

    each(FIRST, "start")

    @pl.when(member == 0)
    def _():
        kbuf[pl.ds(0, WIN), :] = jnp.zeros((WIN, DH), BF16)
        vbuf[pl.ds(0, WIN), :] = jnp.zeros((WIN, DH), BF16)

    each(FIRST, "sent")
    each((K1, V1, QQ1, QQ0), "start")

    def forward():
        pairs = [
            (kbuf.at[first_block], K0), (vbuf.at[first_block], V0),
            (wg, WG), (wu, WU), (wd, WD),
        ]
        return [
            pltpu.make_async_remote_copy(
                ref, ref, fwd_send.at[which], recv.at[which],
                device_id=(x, my_head * per_head), device_id_type=pl.DeviceIdType.MESH,
            )
            for ref, which in pairs
        ]

    @pl.when(member == 1)
    def _():
        if gathered:
            for src, dst, which in ((wg_in, wg, WG), (wu_in, wu, WU), (wd_in, wd, WD)):
                pltpu.make_async_copy(src.at[my_head], dst, recv.at[which]).start()
        arrived(rates, recv.at[RATE])

        def spread(i, carry):
            row = rates[i][0:1, :]
            col = jnp.broadcast_to(row, (128, 128)).T
            rate_col[pl.ds(pl.multiple_of(i * tok, tok), tok), :] = col[:tok]
            return carry

        lax.fori_loop(0, seq_count, spread, 0)
        arrived(kbuf.at[first_block], recv.at[K0])
        arrived(vbuf.at[first_block], recv.at[V0])
        arrived(wg, recv.at[WG])
        arrived(wu, recv.at[WU])
        arrived(wd, recv.at[WD])
        for copy in forward():
            copy.start()

        grads[...] = jnp.zeros_like(grads)

        def grad_tile(i, carry):
            place = pl.ds(pl.multiple_of(WIN + i * TILE, TILE), TILE)
            kn = rms(kbuf[place, :])
            vals = vbuf[place, :]
            gate_pre = dot(kn, wg[...])
            up_pre = dot(kn, wu[...])
            back = dot(vals, wd[...], NT)
            rate = rate_col[pl.ds(pl.multiple_of(i * TILE, TILE), TILE), 0:1]
            sig = jax.nn.sigmoid(gate_pre)
            act = gate_pre * sig
            rate_back = rate * back
            d_gate = (rate_back * up_pre * sig * (1.0 + gate_pre * (1.0 - sig))).astype(BF16)
            d_up = (rate_back * act).astype(BF16)
            h_rate = (rate * act * up_pre).astype(BF16)
            grads[0] += dot(kn, d_gate, TN)
            grads[1] += dot(kn, d_up, TN)
            grads[2] += dot(vals, h_rate, TN)
            return carry

        lax.fori_loop(0, length // TILE, grad_tile, 0)

        for p in range(3):
            g = grads[p]
            total = jnp.sum(jnp.sum(g * g, axis=1, keepdims=True), axis=0, keepdims=True)
            grads[p] = g / (jnp.sqrt(total) + 1e-07)

        def newton(i, carry):
            its = [grads[p] for p in range(3)]
            parts = [split(it) for it in its]
            grams = [dot3(part, part, NT) for part in parts]
            gram_parts = [split(gram) for gram in grams]
            polys = [
                -4.775 * gram + 2.0315 * dot3(gp, gp)
                for gram, gp in zip(grams, gram_parts)
            ]
            for p in range(3):
                grads[p] = 3.4445 * its[p] + dot3(split(polys[p]), parts[p])
            return carry

        lax.fori_loop(0, NS_STEPS, newton, 0)
        for copy in forward():
            copy.wait_send()
        step = step_in[my_head]
        wg[...] = (wg[...].astype(F32) + step * grads[0]).astype(BF16)
        wu[...] = (wu[...].astype(F32) + step * grads[1]).astype(BF16)
        wd[...] = (wd[...].astype(F32) + step * grads[2].T).astype(BF16)
        arrived(kbuf.at[second_block], recv.at[K1])
        arrived(vbuf.at[second_block], recv.at[V1])

    @pl.when(member == 0)
    def _():
        arrived(kbuf.at[first_block], recv.at[K0])
        arrived(vbuf.at[first_block], recv.at[V0])
        arrived(wg, recv.at[WG])
        arrived(wu, recv.at[WU])
        arrived(wd, recv.at[WD])

    @pl.when(owner)
    def _():
        arrived(qbuf, recv.at[QQ0])
        head_column = pl.ds(pl.multiple_of((x * heads_here + my_head) * DH, DH), DH)
        per_tile = TILE // rows

        def tile_step(i, carry):
            place = pl.ds(pl.multiple_of(i * TILE, TILE), TILE)
            q = qbuf[place, :]
            base = member * length + i * TILE
            span = pl.ds(pl.multiple_of(base, TILE), TILE + WIN)
            scores = dot(q, kbuf[span, :], NT) * (1.0 / math.sqrt(DH))
            r = lax.broadcasted_iota(jnp.int32, scores.shape, 0)
            c = lax.broadcasted_iota(jnp.int32, scores.shape, 1)
            gap = r + WIN - c
            allowed = (gap >= 0) & (gap < WIN) & (c + (base - WIN) >= 0)
            scores = jnp.where(allowed, scores, -1e30)
            e = jnp.exp(scores - jnp.max(scores, axis=-1, keepdims=True))
            probs = (e / jnp.sum(e, axis=-1, keepdims=True)).astype(BF16)
            attn = dot(probs, vbuf[span, :])
            qn = rms(q)
            gate = dot(qn, wg[...])
            up = dot(qn, wu[...])
            hidden = (gate * jax.nn.sigmoid(gate) * up).astype(BF16)
            fast = dot(hidden, wd[...])
            obuf[place, :] = (fast + attn).astype(BF16).astype(out_type)

            def ship(j, inner):
                number = i * per_tile + j
                ds, dx = number // head_devices, number % head_devices
                src = obuf.at[pl.ds(pl.multiple_of(number * rows, rows), rows)]
                dst = fin.at[member, :, head_column]
                mine = (ds == s) & (dx == x)

                @pl.when(mine)
                def _():
                    pltpu.make_async_copy(src, dst, recv.at[FIN + member]).start()

                @pl.when(jnp.logical_not(mine))
                def _():
                    pltpu.make_async_remote_copy(
                        src, dst, out_send.at[0], recv.at[FIN + member],
                        device_id=(dx, ds), device_id_type=pl.DeviceIdType.MESH,
                    ).start()

                return inner

            lax.fori_loop(0, per_tile, ship, 0)
            return carry

        lax.fori_loop(0, length // TILE, tile_step, 0)

    each((K1, V1, QQ1, QQ0), "sent")
    for block in range(2):
        arrived(fin.at[block], recv.at[FIN + block])
        wide = fin[block].astype(F32)
        mean_square = jnp.mean(wide * wide, axis=-1, keepdims=True)
        out_ref[block] = (wide * lax.rsqrt(mean_square + 1e-06) * gain_in[...]).astype(BF16)

    @pl.when(owner)
    def _():
        left = obuf.at[pl.ds(0, length - rows)]
        pltpu.make_async_copy(left, left, out_send.at[0]).wait()


def body(queries, keys, values, token_rates, step_size, w_gate, w_up, w_down, norm_gain):
    blocks, tok, width = queries.shape
    heads_here = width // DH
    seq_count = lax.axis_size("seq")
    head_devices = lax.axis_size("head")
    length = tok * seq_count
    rows = tok // head_devices
    gathered = w_gate.shape[1] % 16 != 0
    if gathered:
        w_gate, w_up, w_down = (
            lax.all_gather(w, "seq", axis=1, tiled=True) for w in (w_gate, w_up, w_down)
        )
    out_type = BF16 if rows % 16 == 0 else F32
    rate = jnp.pad(token_rates[0], ((0, 0), (0, 128 - tok)))
    rate = jnp.broadcast_to(rate[:, None, :], (heads_here, 8, 128))
    cfg = (heads_here, seq_count, head_devices, tok, length, gathered, out_type)
    hbm = pl.BlockSpec(memory_space=pl.ANY)
    vmem = pl.BlockSpec(memory_space=pltpu.VMEM)
    smem = pl.BlockSpec(memory_space=pltpu.SMEM)
    return pl.pallas_call(
        functools.partial(kernel, cfg),
        out_shape=jax.ShapeDtypeStruct((blocks, rows, width * head_devices), BF16),
        in_specs=[hbm, hbm, hbm, hbm, smem, hbm, hbm, hbm, vmem],
        out_specs=vmem,
        scratch_shapes=[
            pltpu.VMEM((WIN + 2 * length, DH), BF16),
            pltpu.VMEM((WIN + 2 * length, DH), BF16),
            pltpu.VMEM((length, DH), BF16),
            pltpu.VMEM((DH, DF), BF16),
            pltpu.VMEM((DH, DF), BF16),
            pltpu.VMEM((DF, DH), BF16),
            pltpu.VMEM((seq_count, 8, 128), F32),
            pltpu.VMEM((length, 128), F32),
            pltpu.VMEM((3, DH, DF), F32),
            pltpu.VMEM((length, DH), out_type),
            pltpu.VMEM((2, rows, width * head_devices), out_type),
            pltpu.SemaphoreType.DMA((10, heads_here)),
            pltpu.SemaphoreType.DMA((12,)),
            pltpu.SemaphoreType.DMA((5,)),
            pltpu.SemaphoreType.DMA((1,)),
        ],
        compiler_params=pltpu.CompilerParams(
            has_side_effects=True, vmem_limit_bytes=44 * 1024 * 1024
        ),
    )(
        queries, keys, values, rate, step_size, w_gate, w_up, w_down,
        norm_gain.reshape(1, -1),
    )


def solution(mesh):
    placed = (
        P(None, "seq", "head"),
        P(None, "seq", "head"),
        P(None, "seq", "head"),
        P(None, "head", "seq"),
        P("head"),
        P("head", "seq", None),
        P("head", "seq", None),
        P("head", "seq", None),
        P(),
    )
    return jax.shard_map(
        body, mesh=mesh, in_specs=placed, out_specs=P(None, ("seq", "head"), None), check_vma=False
    )
```

time: 690 us -> 76.3 us (0.11); the launches traced: 678 us -> 76 us
  waiting for transfers between devices: 445 us -> 0 us
  Pallas kernels: 0 us -> 67.9 us
  matrix products: 62.4 us -> 0 us
  local copies, waits for them, and re-layouts: 64.8 us -> 8.04 us
  other arithmetic: 47.5 us -> 0 us
  starting transfers between devices: 32.6 us -> 0 us
  between operations: 15.9 us -> 0.02 us
  blocking collectives: 9.84 us -> 0 us
    psum x2 -> x0, waiting for transfers between devices: 330 us -> none  [the longest x1 192 us: body(): summed = lax.psum(stacked, 'seq')]
    all_gather x3 -> x0, waiting for transfers between devices: 73.6 us -> none  [the longest x1 38 us: body(): lax.all_gather(w_gate, 'seq', axis=1, tiled=True)]
    pallas_call x0 -> x1, Pallas kernels: none -> 67.9 us  [body(): pl.pallas_call(functools.partial(kernel, cfg), out_shape=jax.ShapeDtypeSt...]
    dot_general x42 -> x0, matrix products: 62.4 us -> none  [the longest x10 11.8 us: newton(): jnp.dot(poly, iterate, precision=lax.Precision.HIGHEST, preferred_element...]
    ppermute x16 -> x0, waiting for transfers between devices: 40.6 us -> none  [shifted(): lax.ppermute(array, axis, [(i, (i + by) % count) for i in range(count)])]
    ppermute x16 -> x0, starting transfers between devices: 32.5 us -> none  [shifted(): lax.ppermute(array, axis, [(i, (i + by) % count) for i in range(count)])]
    slice x17 -> x0, local copies, waits for them, and re-layouts: 26 us -> none  [the longest x16 25 us: body(): before = jnp.concatenate([jnp.zeros_like(part_arr[:1]), part_arr[:-1]], 0)]
    unnamed x15 -> x0, other arithmetic: 24.5 us -> none
  transfers between devices with their start and end apart: 21 -> 0, of which waited for: 16 -> 0; matrix products, arithmetic and copies ran while one was open for 16% -> 0% of each run, Pallas kernels for 0% -> 0%
where the time goes in v1:
time: 76.3 us; the launch traced here: 76 us
  Pallas kernels  67.9 us (89%)
  local copies, waits for them, and re-layouts  8.04 us (11%)
    pallas_call x1, Pallas kernels, body(): pl.pallas_call(functools.partial(kernel, cfg), out_shape=jax.ShapeDtypeSt...  67.9 us
    unnamed x17, local copies, waits for them, and re-layouts  7.34 us

profile of v1, /device:TPU:25, one launch (start us, length us, event | category | flops | bytes accessed | tf_op | source)
XLA Modules:
  0.0 76.0 jit_solution(4367988843890418715)
XLA Ops:
  0.0 0.7 pad.4
  0.7 0.0 copy-start.6
  0.7 0.0 copy-start.7
  0.7 0.7 copy-done.6
  1.4 0.0 copy-done.7
  1.4 0.0 copy-start
  1.4 1.0 %copy-done = bf16[2,64,2048]{2,1,0:T(8,128)(2,1)S(1)} copy-done((bf16[2,64,2048]{2,1,0:T(8,128)(2,1)S(1)}, bf16[2,64,2048]{2,1,0:T(8,128)(2,1)}, u32[]{:S(2)}) %copy-start) | copy-done | bytes 524312
  2.5 0.0 copy-start.1
  2.5 1.0 %copy-done.1 = bf16[2,64,2048]{2,1,0:T(8,128)(2,1)S(1)} copy-done((bf16[2,64,2048]{2,1,0:T(8,128)(2,1)S(1)}, bf16[2,64,2048]{2,1,0:T(8,128)(2,1)}, u32[]{:S(2)}) %copy-start.1) | copy-done | bytes 524312
  3.5 0.0 copy-start.2
  3.5 1.0 %copy-done.2 = bf16[2,64,2048]{2,1,0:T(8,128)(2,1)S(1)} copy-done((bf16[2,64,2048]{2,1,0:T(8,128)(2,1)S(1)}, bf16[2,64,2048]{2,1,0:T(8,128)(2,1)}, u32[]{:S(2)}) %copy-start.2) | copy-done | bytes 524312
  4.5 0.0 copy-start.3
  4.5 0.9 %copy-done.3 = bf16[8,16,512]{2,1,0:T(8,128)(2,1)S(1)} copy-done((bf16[8,16,512]{2,1,0:T(8,128)(2,1)S(1)}, bf16[8,16,512]{2,1,0:T(8,128)(2,1)}, u32[]{:S(2)}) %copy-start.3) | copy-done | bytes 131096
  5.4 0.0 copy-start.4
  5.4 0.9 %copy-done.4 = bf16[8,16,512]{2,1,0:T(8,128)(2,1)S(1)} copy-done((bf16[8,16,512]{2,1,0:T(8,128)(2,1)S(1)}, bf16[8,16,512]{2,1,0:T(8,128)(2,1)}, u32[]{:S(2)}) %copy-start.4) | copy-done | bytes 131096
  6.3 0.0 copy-start.5
  6.4 0.9 %copy-done.5 = bf16[8,32,256]{2,1,0:T(8,128)(2,1)S(1)} copy-done((bf16[8,32,256]{2,1,0:T(8,128)(2,1)S(1)}, bf16[8,32,256]{2,1,0:T(8,128)(2,1)}, u32[]{:S(2)}) %copy-start.5) | copy-done | bytes 131096
  7.3 67.9 %shard_map.91 = bf16[2,32,4096]{2,1,0:T(8,128)(2,1)S(1)} custom-call(bf16[2,64,2048]{2,1,0:T(8,128)(2,1)S(1)} %copy-done, bf16[2,64,2048]{2,1,0:T(8,128)(2,1)S(1)} %copy-done.1, bf16[2,64,2048]{2,1,0:T(8,128)(2,1)S(1)} %copy-done.2, f32[8,8,128]{2,1,0:T(8,128)S(1)} %broadcast_in_dim.2.refs_3_, f32[8]{0:T(128)S(1)} %copy-done.7, ...), custom_call_target="tpu_custom_call" | custom-call | tf_op jit(solution)/shard_map/pallas_call | solution.py:316
  75.2 0.8 %copy.11 = bf16[2,32,4096]{2,1,0:T(8,128)(2,1)} copy(bf16[2,32,4096]{2,1,0:T(8,128)(2,1)S(1)} %shard_map.91) | data formatting | bytes 1048576
  (1 shorter events, 0.0 us)
Async XLA Ops:
  0.7 0.7 copy-start.6
  0.7 0.7 copy-start.7
  1.4 1.0 %copy-start = (bf16[2,64,2048]{2,1,0:T(8,128)(2,1)S(1)}, bf16[2,64,2048]{2,1,0:T(8,128)(2,1)}, u32[]{:S(2)}) copy-start(bf16[2,64,2048]{2,1,0:T(8,128)(2,1)} %refs_0_.1) | copy-start | bytes 1572868
  2.5 1.0 %copy-start.1 = (bf16[2,64,2048]{2,1,0:T(8,128)(2,1)S(1)}, bf16[2,64,2048]{2,1,0:T(8,128)(2,1)}, u32[]{:S(2)}) copy-start(bf16[2,64,2048]{2,1,0:T(8,128)(2,1)} %refs_1_.1) | copy-start | bytes 1572868
  3.5 1.0 %copy-start.2 = (bf16[2,64,2048]{2,1,0:T(8,128)(2,1)S(1)}, bf16[2,64,2048]{2,1,0:T(8,128)(2,1)}, u32[]{:S(2)}) copy-start(bf16[2,64,2048]{2,1,0:T(8,128)(2,1)} %refs_2_.1) | copy-start | bytes 1572868
  4.5 0.9 %copy-start.3 = (bf16[8,16,512]{2,1,0:T(8,128)(2,1)S(1)}, bf16[8,16,512]{2,1,0:T(8,128)(2,1)}, u32[]{:S(2)}) copy-start(bf16[8,16,512]{2,1,0:T(8,128)(2,1)} %refs_5_.1) | copy-start | bytes 393220
  5.4 0.9 %copy-start.4 = (bf16[8,16,512]{2,1,0:T(8,128)(2,1)S(1)}, bf16[8,16,512]{2,1,0:T(8,128)(2,1)}, u32[]{:S(2)}) copy-start(bf16[8,16,512]{2,1,0:T(8,128)(2,1)} %refs_6_.1) | copy-start | bytes 393220
  6.3 0.9 %copy-start.5 = (bf16[8,32,256]{2,1,0:T(8,128)(2,1)S(1)}, bf16[8,32,256]{2,1,0:T(8,128)(2,1)}, u32[]{:S(2)}) copy-start(bf16[8,32,256]{2,1,0:T(8,128)(2,1)} %refs_7_.1) | copy-start | bytes 393220

commit v2 on v1

--- a/solution.py
+++ b/solution.py
@@ -41,6 +41,16 @@
     wide = tile.astype(F32)
     mean_square = jnp.mean(wide * wide, axis=-1, keepdims=True)
     return (wide * lax.rsqrt(mean_square + 1e-06)).astype(BF16)
+
+
+def partner(head, number, count):
+    if count & (count - 1):
+        return (head + number) % count
+    other, bit = 0, 1
+    while bit < count:
+        other = other + bit * ((head // bit + number // bit) % 2)
+        bit *= 2
+    return other
 
 
 def kernel(cfg, *refs):
@@ -56,6 +66,20 @@
     rows = tok // head_devices
     g_rows = DH // seq_count
     d_rows = DF // seq_count
+
+    total = seq_count * head_devices
+    barrier = pltpu.get_barrier_semaphore()
+
+    def greet(i, carry):
+        other = (x * seq_count + s + 1 + i) % total
+        pl.semaphore_signal(
+            barrier, inc=1, device_id=(other // seq_count, other % seq_count),
+            device_id_type=pl.DeviceIdType.MESH,
+        )
+        return carry
+
+    lax.fori_loop(0, total - 1, greet, 0)
+    pl.semaphore_wait(barrier, total - 1)
 
     def at_rows(ref, start, size, step):
         return ref.at[pl.ds(pl.multiple_of(start, step), size)]
@@ -90,7 +114,7 @@
 
     def each(which_list, action):
         def one(j, carry):
-            h = (my_head + j) % heads_here
+            h = partner(my_head, heads_here - 1 - j, heads_here)
             for which in which_list:
                 if gathered and which in (WG, WU, WD):
                     continue
@@ -132,7 +156,6 @@
         kbuf[pl.ds(0, WIN), :] = jnp.zeros((WIN, DH), BF16)
         vbuf[pl.ds(0, WIN), :] = jnp.zeros((WIN, DH), BF16)
 
-    each(FIRST, "sent")
     each((K1, V1, QQ1, QQ0), "start")
 
     def forward():
@@ -281,7 +304,7 @@
 
         lax.fori_loop(0, length // TILE, tile_step, 0)
 
-    each((K1, V1, QQ1, QQ0), "sent")
+    each((K1, V1, QQ1, QQ0) + FIRST, "sent")
     for block in range(2):
         arrived(fin.at[block], recv.at[FIN + block])
         wide = fin[block].astype(F32)
@@ -310,7 +333,7 @@
     rate = jnp.pad(token_rates[0], ((0, 0), (0, 128 - tok)))
     rate = jnp.broadcast_to(rate[:, None, :], (heads_here, 8, 128))
     cfg = (heads_here, seq_count, head_devices, tok, length, gathered, out_type)
-    hbm = pl.BlockSpec(memory_space=pl.ANY)
+    hbm = pl.BlockSpec(memory_space=pltpu.HBM)
     vmem = pl.BlockSpec(memory_space=pltpu.VMEM)
     smem = pl.BlockSpec(memory_space=pltpu.SMEM)
     return pl.pallas_call(
@@ -336,7 +359,7 @@
             pltpu.SemaphoreType.DMA((1,)),
         ],
         compiler_params=pltpu.CompilerParams(
-            has_side_effects=True, vmem_limit_bytes=44 * 1024 * 1024
+            has_side_effects=True, collective_id=0, vmem_limit_bytes=63 * 1024 * 1024
         ),
     )(
         queries, keys, values, rate, step_size, w_gate, w_up, w_down,

time: 76.3 us -> 70.1 us (0.919)
  local copies, waits for them, and re-layouts: 8.04 us -> 3.18 us
  Pallas kernels: 67.9 us -> 65.9 us
    unnamed x17 -> x1, local copies, waits for them, and re-layouts: 7.34 us -> 1.87 us
    pallas_call x1, Pallas kernels: 67.9 us -> 65.9 us  [body(): pl.pallas_call(functools.partial(kernel, cfg), out_shape=jax.ShapeDtypeSt...]
where the time goes in v2:
time: 70.1 us; the launch traced here: 69.1 us
  Pallas kernels  65.9 us (94%)
  local copies, waits for them, and re-layouts  3.18 us (5%)
    pallas_call x1, Pallas kernels, body(): pl.pallas_call(functools.partial(kernel, cfg), out_shape=jax.ShapeDtypeSt...  65.9 us
    unnamed x1, local copies, waits for them, and re-layouts  1.87 us

profile of v2, /device:TPU:25, one launch (start us, length us, event | category | flops | bytes accessed | tf_op | source)
XLA Modules:
  0.0 69.1 jit_solution(3500126029598385358)
XLA Ops:
  0.0 0.7 pad.4
  0.7 0.6 broadcast_in_dim.2.refs_3_
  1.3 65.9 %shard_map.91 = bf16[2,32,4096]{2,1,0:T(8,128)(2,1)} custom-call(bf16[2,64,2048]{2,1,0:T(8,128)(2,1)} %refs_0_.1, bf16[2,64,2048]{2,1,0:T(8,128)(2,1)} %refs_1_.1, bf16[2,64,2048]{2,1,0:T(8,128)(2,1)} %refs_2_.1, f32[8,8,128]{2,1,0:T(8,128)} %broadcast_in_dim.2.refs_3_, f32[8]{0:T(128)} %refs_4_.1, bf16[8,16,512]{2,1,0:T(8,128)(2,1)} %refs_5_.1, ...), custom_call_target="tpu_custom_call" | custom-call | tf_op jit(solution)/shard_map/pallas_call | solution.py:339
  67.3 1.9 %copy.11 = bf16[2,32,4096]{2,1,0:T(8,128)(2,1)} copy(bf16[2,32,4096]{2,1,0:T(8,128)(2,1)} %shard_map.91) | data formatting | bytes 1048576
